TPU v7x, 32 devices: a whole 2x2x4 slice. The times are simulated.
32 devices in a mesh: fsdp: 16 (over z, y, core), row: 2 (over x).
Axes of the slice: x: 2, y: 2, z: 4, core: 2. Of those that a mesh axis runs over, the one named last changes fastest.
Arguments:
- factor: float32 [3072, 3072], P('fsdp', 'row'), may hold values from -1 to 17, as said below
- gradient: bfloat16 [3072, 3840], P('row', 'fsdp'), may hold values from -0.125 to 0.125
- sketch_ids: int32 [3072, 256], P('row'), may hold values from -3 to 3
Outputs:
- factor_new: float32 [3072, 3072], P('fsdp', 'row')
- range_basis: float32 [3072, 256], P('fsdp')
- projected_core: float32 [256, 256], replicated
Inputs may be any that keep to these rules, and one draw needn't show every extreme that they name: `factor`: symmetric.
All inputs are finite; a program needn't handle non-finite values.
Results may differ from a plain program's by a relative error of at most 0.0003.
Values may be sent and summed in bfloat16 or wider, within the bound.
A program may use at most 64 MiB of HBM per device.

v0:
```python
import jax
import jax.numpy as jnp
from jax import lax
from jax.sharding import PartitionSpec as P

B = 3072


decay_rate = 0.9


def from_root(block, axis, owner):
    block = jnp.where(lax.axis_index(axis) == owner, block, jnp.zeros_like(block))
    return lax.psum(block, axis)


def shards(factor, gradient, sketch_ids):
    highest = lax.Precision.HIGHEST
    rows_here = factor.shape[0]
    cols_here = factor.shape[1]
    row_pos = lax.axis_index("row")
    fsdp_pos = lax.axis_index("fsdp")
    contract_last = (((1,), (1,)), ((), ()))
    block_rows = lax.all_gather(gradient, "fsdp", axis=1, tiled=True)
    owner = fsdp_pos * rows_here // cols_here
    local_start = jnp.clip(fsdp_pos * rows_here - row_pos * cols_here, 0, cols_here - rows_here)
    own_slice = lax.dynamic_slice_in_dim(block_rows, local_start, rows_here, 0)
    own_slice = from_root(own_slice, "row", owner)
    outer_sum = lax.dot_general(
        own_slice, block_rows, contract_last, preferred_element_type=jnp.float32
    )
    factor_new = decay_rate * factor + outer_sum
    sketch = sketch_ids.astype(jnp.float32)
    ranged = lax.psum(jnp.dot(factor_new, sketch, precision=highest), "row")
    gram_matrix = lax.psum(jnp.dot(ranged.T, ranged, precision=highest), "fsdp") / B
    lower_factor = jnp.linalg.cholesky(gram_matrix)
    range_basis = jax.scipy.linalg.solve_triangular(lower_factor, ranged.T, lower=True).T
    gathered_piece = lax.all_gather(range_basis, "fsdp", axis=0, tiled=True)
    local_cols = jnp.arange(gathered_piece.shape[0], dtype=jnp.int32) - row_pos * cols_here
    inside = ((local_cols >= 0) & (local_cols < cols_here)).astype(jnp.float32)
    picked = jnp.take(factor_new, jnp.clip(local_cols, 0, cols_here - 1), axis=1) * inside[None, :]
    applied = jnp.dot(picked, gathered_piece, precision=highest)
    core_term = jnp.dot(range_basis.T, applied, precision=highest)
    projected_core = lax.psum(core_term, ("fsdp", "row")) / B
    return (factor_new, range_basis, projected_core)


def solution(mesh):
    return jax.shard_map(
        shards,
        mesh=mesh,
        in_specs=(P("fsdp", "row"), P("row", "fsdp"), P("row", None)),
        out_specs=(P("fsdp", "row"), P("fsdp", None), P()),
        check_vma=False,
    )
```

profile of v0, /device:TPU:0, one launch (start us, length us, event | category | flops | bytes accessed | tf_op | source)
XLA Modules:
  0.0 548.9 jit_solution(18035804898174343418)
XLA Ops:
  7.2 0.0 all-gather.3.cloned.1.call-start
  7.2 0.7 all-gather.3.cloned.1.call-update
  7.9 0.0 all-reduce.6.cloned.1.call-start
  8.0 101.0 %all-gather.3.cloned.1.call-done = bf16[1536,3840]{0,1:T(8,128)(2,1)} async-done(((bf16[1536,240]{0,1:T(8,128)(2,1)}), bf16[1536,3840]{0,1:T(8,128)(2,1)}) %all-gather.3.cloned.1.call-update) | async-done | bytes 11796496 | tf_op jit(solution)/shard_map/all_gather | solution.py:24
  108.9 4.3 dynamic-slice_select_fusion
  113.3 0.0 all-reduce.6.cloned.1.call-update
  113.3 0.0 copy-start.2
  113.3 0.0 all-reduce.8.cloned.1.call-start
  113.4 58.3 %all-reduce.6.cloned.1.call-done = bf16[192,3840]{0,1:T(8,128)(2,1)} async-done(((bf16[192,3840]{0,1:T(8,128)(2,1)}), bf16[192,3840]{0,1:T(8,128)(2,1)}) %all-reduce.6.cloned.1.call-update) | async-done | bytes 1474576 | tf_op jit(solution)/shard_map/psum | solution.py:14
  171.7 7.7 %convolution_add_fusion = f32[192,1536]{1,0:T(8,128)S(1)} fusion(bf16[192,3840]{0,1:T(8,128)(2,1)} %all-reduce.6.cloned.1.call-done, bf16[1536,3840]{0,1:T(8,128)(2,1)} %all-gather.3.cloned.1.call-done, f32[192,1536]{1,0:T(8,128)} %param.3), kind=kOutput, calls=%fused_computation.6 | convolution fusion | flops 2265513984 | bytes 15630336 | tf_op jit(solution)/shard_map/dot_general | solution.py:29
  179.3 0.0 copy-done.2
  179.4 0.0 copy-start
  179.4 1.9 fusion.5
  181.2 0.0 all-reduce.8.cloned.1.call-update
  181.3 0.0 all-reduce.10.cloned.1.call-start
  181.3 22.4 %all-reduce.8.cloned.1.call-done = f32[192,256]{1,0:T(8,128)} async-done(((f32[192,256]{1,0:T(8,128)}), f32[192,256]{1,0:T(8,128)}) %all-reduce.8.cloned.1.call-update) | async-done | bytes 196624 | tf_op jit(solution)/shard_map/psum | solution.py:34
  203.8 2.4 fusion.28
  206.1 0.0 all-reduce.10.cloned.1.call-update
  206.2 0.2 all-gather.5.cloned.1.call-start
  206.4 90.3 %all-reduce.10.cloned.1.call-done = f32[256,256]{0,1:T(8,128)} async-done(((f32[256,256]{0,1:T(8,128)}), f32[256,256]{0,1:T(8,128)}) %all-reduce.10.cloned.1.call-update) | async-done | bytes 262160 | tf_op jit(solution)/shard_map/psum | solution.py:35
  296.7 1.0 broadcast_multiply_fusion.1
  297.7 0.0 copy-start.1
  297.7 0.1 copy.12
  297.8 1.0 fusion.8
  298.8 11.7 %cholesky.50 = f32[128,128]{1,0:T(8,128)S(1)} custom-call(f32[128,128]{1,0:T(8,128)S(1)} %cholesky.118), custom_call_target="Cholesky" | custom-call | tf_op jit(solution)/shard_map/jit(cholesky)/cholesky | solution.py:36
  310.6 9.8 %custom-call.15 = f32[1,128,128]{1,2,0:T(8,128)S(1)} custom-call(f32[1,128,128]{2,1,0:T(8,128)S(1)} %get-tuple-element.30), custom_call_target="InvertDiagBlocksLowerTriangular" | custom-call | tf_op jit(solution)/shard_map/jit(cholesky)/cholesky | solution.py:36
  320.4 0.2 constant_dynamic-update-slice_fusion.1
  320.6 0.3 convolution_subtract_fusion.1
  320.9 11.7 %cholesky.105 = f32[128,128]{1,0:T(8,128)S(1)} custom-call(f32[128,128]{1,0:T(8,128)S(1)} %convolution_subtract_fusion.1), custom_call_target="Cholesky" | custom-call | tf_op jit(solution)/shard_map/jit(cholesky)/cholesky | solution.py:36
  332.6 0.6 compare_reduce_fusion
  334.6 0.1 triangular_solve.57
  334.7 4.2 while.1
  334.9 0.6 fusion.41
  335.5 1.4 bitcast_dynamic-update-slice_fusion.2
  336.9 0.6 fusion.41
  337.5 1.4 bitcast_dynamic-update-slice_fusion.2
  338.9 19.7 %custom-call.16 = f32[2,128,128]{1,2,0:T(8,128)S(1)} custom-call(f32[2,128,128]{2,1,0:T(8,128)S(1)} %get-tuple-element.10), custom_call_target="InvertDiagBlocksLowerTriangular" | custom-call | tf_op jit(solution)/shard_map/jit(_solve_triangular)/triangular_solve | solution.py:37
  358.5 0.0 copy-done.1
  358.6 0.2 fusion.11
  358.8 0.3 convolution_subtract_fusion
  359.1 0.2 fusion.14
  359.3 0.7 fusion.10
  360.0 0.0 all-gather.5.cloned.1.call-update
  360.0 0.0 all-reduce.12.cloned.1.call-start
  360.2 0.0 copy-done
  360.2 0.5 copy.13
  360.6 12.4 %gather_fusion = f32[3072,192]{1,0:T(8,128)} fusion(f32[192,1536]{0,1:T(8,128)S(1)} %copy.13, s32[3072]{0:T(1024)S(1)} %broadcast_clamp_fusion), kind=kCustom, calls=%fused_computation | custom fusion | bytes 4730880 | tf_op jit(solution)/shard_map/jit(_take)/gather | solution.py:41
  373.0 32.8 %all-gather.5.cloned.1.call-done = f32[3072,256]{1,0:T(8,128)} async-done(((f32[192,256]{1,0:T(8,128)}), f32[3072,256]{1,0:T(8,128)}) %all-gather.5.cloned.1.call-update) | async-done | bytes 3145744 | tf_op jit(solution)/shard_map/all_gather | solution.py:38
  405.9 9.0 %fusion = f32[192,256]{1,0:T(8,128)S(1)} fusion(f32[3072,256]{1,0:T(8,128)} %all-gather.5.cloned.1.call-done, f32[3072,192]{1,0:T(8,128)} %gather_fusion, f32[3072]{0:T(1024)S(1)} %get-tuple-element.34, pred[3072]{0:T(1024)(128)(4,1)S(1)} %get-tuple-element.33), kind=kOutput, calls=%fused_computation.3 | convolution fusion | flops 1813118976 | bytes 5716992 | tf_op jit(solution)/shard_map/dot_general | solution.py:42
  414.9 1.4 fusion.9
  416.2 0.0 all-reduce.12.cloned.1.call-update
  416.3 123.9 %all-reduce.12.cloned.1.call-done = f32[256,256]{0,1:T(8,128)} async-done(((f32[256,256]{0,1:T(8,128)}), f32[256,256]{0,1:T(8,128)}) %all-reduce.12.cloned.1.call-update) | async-done | bytes 262160 | tf_op jit(solution)/shard_map/psum | solution.py:44
  540.2 1.0 broadcast_multiply_fusion
  541.2 0.8 copy.15
  (12 shorter events, 0.2 us)
Async XLA Ops:
  7.2 101.8 %all-gather.3.cloned.1.call-start = ((), (), s32[]{:S(2)}) async-start(), calls=%async_computation | async-start | bytes 12533760 | tf_op jit(solution)/shard_map/all_gather | solution.py:24
  7.9 163.8 %all-reduce.6.cloned.1.call-start = ((), (), s32[]{:S(2)}) async-start(), calls=%async_computation.1 | async-start | bytes 3932160 | tf_op jit(solution)/shard_map/psum | solution.py:14
  113.3 66.0 %copy-start.2 = (s32[1536,256]{1,0:T(8,128)S(1)}, s32[1536,256]{1,0:T(8,128)}, u32[]{:S(2)}) copy-start(s32[1536,256]{1,0:T(8,128)} %param.5) | copy-start | bytes 4718596
  113.3 90.4 %all-reduce.8.cloned.1.call-start = ((), (), s32[]{:S(2)}) async-start(), calls=%async_computation.2 | async-start | bytes 393216 | tf_op jit(solution)/shard_map/psum | solution.py:34
  179.4 180.8 %copy-start = (f32[192,1536]{1,0:T(8,128)}, f32[192,1536]{1,0:T(8,128)S(1)}, u32[]{:S(2)}) copy-start(f32[192,1536]{1,0:T(8,128)S(1)} %convolution_add_fusion) | copy-start | bytes 3538948
  181.3 115.4 %all-reduce.10.cloned.1.call-start = ((), (), s32[]{:S(2)}) async-start(), calls=%async_computation.3 | async-start | bytes 524288 | tf_op jit(solution)/shard_map/psum | solution.py:35
  206.2 199.7 %all-gather.5.cloned.1.call-start = ((), (), s32[]{:S(2)}) async-start(), calls=%async_computation.4 | async-start | bytes 3342336 | tf_op jit(solution)/shard_map/all_gather | solution.py:38
  297.7 60.9 %copy-start.1 = (f32[192,256]{1,0:T(8,128)S(1)}, f32[192,256]{1,0:T(8,128)}, u32[]{:S(2)}) copy-start(f32[192,256]{1,0:T(8,128)} %all-reduce.8.cloned.1.call-done) | copy-start | bytes 589828
  360.0 180.2 %all-reduce.12.cloned.1.call-start = ((), (), s32[]{:S(2)}) async-start(), calls=%async_computation.5 | async-start | bytes 524288 | tf_op jit(solution)/shard_map/psum | solution.py:44
Sparse Core Ops, SparseCore 0:
  10.3 98.6 all-gather.2
  113.4 58.2 all-reduce.5
  181.4 22.3 all-reduce.7
  207.9 88.6 all-reduce.9
  360.2 45.6 all-gather.4
  416.4 123.7 all-reduce.11
where the time goes:
time: 549 us
  waiting for transfers between devices  430 us (78%)
  other arithmetic  61.7 us (11%)
  matrix products  23.5 us (4%)
  local copies, waits for them, and re-layouts  17.9 us (3%)
  between operations  15.6 us (3%)
    psum x1, waiting for transfers between devices, shards(): projected_core = lax.psum(core_term, ('fsdp', 'row')) / B  124 us
    all_gather x1, waiting for transfers between devices, shards(): block_rows = lax.all_gather(gradient, 'fsdp', axis=1, tiled=True)  101 us
    psum x1, waiting for transfers between devices, shards(): lax.psum(jnp.dot(ranged.T, ranged, precision=highest), 'fsdp') / B  90.3 us
    psum x1, waiting for transfers between devices, from_root(): return lax.psum(block, axis)  58.3 us
    another operation x6, other arithmetic, shards(): lower_factor = jnp.linalg.cholesky(gram_matrix)  34 us
    all_gather x1, waiting for transfers between devices, shards(): gathered_piece = lax.all_gather(range_basis, 'fsdp', axis=0, tiled=True)  32.8 us
    psum x1, waiting for transfers between devices, shards(): ranged = lax.psum(jnp.dot(factor_new, sketch, precision=highest), 'row')  22.4 us
    another operation x3, other arithmetic, shards(): jax.scipy.linalg.solve_triangular(lower_factor, ranged.T, lower=True)  19.7 us
  transfers between devices with their start and end apart: 6, of which 6 were waited for; matrix products, arithmetic and copies ran while one was open for 2% of the time, Pallas kernels for 0%

commit v1 on v0

v1 whole, which is shorter than its diff:
```python
import functools

import jax
import jax.numpy as jnp
from jax import lax
from jax.experimental import pallas as pl
from jax.experimental.pallas import tpu as pltpu
from jax.sharding import PartitionSpec as P

decay_rate = 0.9
HIGHEST = lax.Precision.HIGHEST
MESH = pl.DeviceIdType.MESH
VMEM_BYTES = 52 * 1024 * 1024
NB = 64


def nt(a, b, precision=None):
    return lax.dot_general(a, b, (((1,), (1,)), ((), ())), precision=precision, preferred_element_type=jnp.float32)


def nn(a, b, precision=None):
    return lax.dot_general(a, b, (((1,), (0,)), ((), ())), precision=precision, preferred_element_type=jnp.float32)


def tn(a, b, precision=None):
    return lax.dot_general(a, b, (((0,), (0,)), ((), ())), precision=precision, preferred_element_type=jnp.float32)


def split(a):
    high = a.astype(jnp.bfloat16)
    return high, (a - high.astype(jnp.float32)).astype(jnp.bfloat16)


def place():
    f = lax.axis_index("fsdp")
    return f, lax.axis_index("row"), f // 4, (f // 2) % 2, f % 2


def relay(buf, slot, has, nz, send_sem, recv_sem, on_piece):
    f, x, z, y, c = place()

    def copy(piece, kind, target):
        return pltpu.make_async_remote_copy(
            src_ref=buf.at[slot(piece)], dst_ref=buf.at[slot(piece)],
            send_sem=send_sem.at[kind, slot(piece)], recv_sem=recv_sem.at[slot(piece)],
            device_id={"fsdp": target, "row": x}, device_id_type=MESH)

    def each(source, go, act):
        @pl.when(go)
        def _():
            piece = source * 4 + y * 2 + c

            @pl.when((source <= z) & (z + 1 < nz))
            def _():
                act(copy(piece, 0, f + 4))

            @pl.when((source >= z) & (z > 0))
            def _():
                act(copy(piece, 1, f - 4))

            act(copy(piece, 2, f + 2 - 4 * y))
            act(copy(piece, 3, f + 1 - 2 * c))

    def across(source, go, act):
        @pl.when(go)
        def _():
            act(copy(source * 4 + (1 - y) * 2 + c, 3, f + 1 - 2 * c))

    def at_distance(d):
        out = []
        for s in ([0] if d == 0 else [-d, d]):
            source = z + s
            ok = (source >= 0) & (source < nz)
            safe = jnp.clip(source, 0, nz - 1)
            out.append((safe, ok & has(safe)))
        return out

    def arrive(piece):
        copy(piece, 0, f + 1 - 2 * c).wait_recv()

    for stage in range(nz + 1):
        own = at_distance(stage) if stage < nz else []
        far = at_distance(stage - 1) if stage > 0 else []
        for source, go in own:
            if stage > 0:
                @pl.when(go)
                def _(source=source):
                    arrive(source * 4 + y * 2 + c)
            each(source, go, lambda op: op.start())
        for source, go in far:
            @pl.when(go)
            def _(source=source):
                arrive(source * 4 + (1 - y) * 2 + c)
            across(source, go, lambda op: op.start())
        for sources, side in ((own, y), (far, 1 - y)):
            for source, go in sources:
                @pl.when(go)
                def _(source=source, side=side):
                    on_piece(source * 4 + side * 2 + c)
                    other = source * 4 + side * 2 + 1 - c
                    arrive(other)
                    on_piece(other)

    def finish():
        for stage in range(nz):
            for source, go in at_distance(stage):
                each(source, go, lambda op: op.wait_send())
                across(source, go, lambda op: op.wait_send())

    return finish


def main_kernel(nz, factor_ref, grad_ref, sketch_ref, new_ref, range_ref, gram_ref, term_ref,
                grad_buf, own_buf, half_buf, range_buf, gram_buf,
                g_send, g_recv, o_send, o_recv, r_send, r_recv, x_send, x_recv, load_sem):
    f, x, z, y, c = place()
    rows, cols = factor_ref.shape
    per = cols // rows
    mine = (f // per) == x
    start = pl.multiple_of(jnp.clip(f - x * per, 0, per - 1) * rows, rows)
    load = pltpu.make_async_copy(grad_ref, grad_buf.at[f], load_sem)
    load.start()

    barrier = pltpu.get_barrier_semaphore()

    def hello(target, row):
        pl.semaphore_signal(barrier, inc=1, device_id={"fsdp": target, "row": row}, device_id_type=MESH)

    hello(f, 1 - x)
    hello(f + 1 - 2 * c, x)
    hello(f + 2 - 4 * y, x)

    @pl.when(z > 0)
    def _():
        hello(f - 4, x)

    @pl.when(z + 1 < nz)
    def _():
        hello(f + 4, x)

    pl.semaphore_wait(barrier, 3 + jnp.where(z > 0, 1, 0) + jnp.where(z + 1 < nz, 1, 0))

    def over_x(src, dst, send, recv):
        return pltpu.make_async_remote_copy(
            src_ref=src, dst_ref=dst, send_sem=send, recv_sem=recv,
            device_id={"fsdp": f, "row": 1 - x}, device_id_type=MESH)

    def own_copy(piece):
        return over_x(own_buf.at[piece], own_buf.at[piece], o_send.at[piece], o_recv.at[piece])

    load.wait()
    new_ref[...] = decay_rate * factor_ref[...]

    def on_grad(piece):
        @pl.when(mine)
        def _():
            own_buf[piece] = grad_buf[piece, pl.ds(start, rows), :]
            own_copy(piece).start()

        @pl.when(jnp.logical_not(mine))
        def _():
            own_copy(piece).wait_recv()

        new_ref[...] += nt(own_buf[piece], grad_buf[piece])

    finish_grad = relay(grad_buf, lambda p: p, lambda s: s >= 0, nz, g_send, g_recv, on_grad)

    new_high, new_low = split(new_ref[...])
    sketch = sketch_ref[...].astype(jnp.float32).astype(jnp.bfloat16)
    half_buf[0] = nn(new_high, sketch) + nn(new_low, sketch)
    trade = over_x(half_buf.at[0], half_buf.at[1], x_send.at[0], x_recv.at[0])
    trade.start()
    trade.wait()
    ranged = half_buf[0] + half_buf[1]
    range_ref[...] = ranged

    @pl.when(mine)
    def _():
        range_buf[jnp.clip(f - x * per, 0, per - 1)] = ranged

    finish_range = relay(
        range_buf, lambda p: jnp.clip(p - x * per, 0, per - 1),
        lambda s: ((s * 4) // per) == x, nz, r_send, r_recv, lambda p: None)

    meet = range_buf[...].reshape(cols, ranged.shape[1])
    meet_high, meet_low = split(meet)
    cross = tn(meet_high, meet_low)
    gram_buf[0] = tn(meet_high, meet_high) + cross + tn(meet_low, meet_high)
    trade_gram = over_x(gram_buf.at[0], gram_buf.at[1], x_send.at[1], x_recv.at[1])
    trade_gram.start()
    applied = nn(new_high, meet_high) + nn(new_low, meet_high) + nn(new_high, meet_low)
    applied_high, applied_low = split(applied)
    ranged_high, ranged_low = split(range_ref[...])
    term_ref[...] = tn(ranged_high, applied_high) + tn(ranged_low, applied_high) + tn(ranged_high, applied_low)
    trade_gram.wait()
    gram_ref[...] = gram_buf[0] + gram_buf[1]

    finish_grad()
    finish_range()

    @pl.when(mine)
    def _():
        for piece in range(4 * nz):
            own_copy(piece).wait_send()


def sum_kernel(total, term_ref, out_ref, parts, send_a, recv_a, send_b, recv_b):
    me = lax.axis_index("fsdp") * 2 + lax.axis_index("row")
    chunk = term_ref.shape[0] // total

    def where(k):
        t = lax.rem(me + k, total)
        return t, {"fsdp": t // 2, "row": lax.rem(t, 2)}

    barrier = pltpu.get_barrier_semaphore()

    def greet(k, _):
        pl.semaphore_signal(barrier, inc=1, device_id=where(k)[1], device_id_type=MESH)
        return 0

    lax.fori_loop(1, total, greet, 0)
    pl.semaphore_wait(barrier, total - 1)

    def rows_of(t):
        return pl.ds(pl.multiple_of(t * chunk, chunk), chunk)

    def scatter(k):
        t, device = where(k)
        return pltpu.make_async_remote_copy(
            src_ref=term_ref.at[rows_of(t)], dst_ref=parts.at[me],
            send_sem=send_a.at[t], recv_sem=recv_a.at[me], device_id=device, device_id_type=MESH)

    def scattered(k):
        t, device = where(k)
        return pltpu.make_async_remote_copy(
            src_ref=term_ref.at[rows_of(t)], dst_ref=parts.at[t],
            send_sem=send_a.at[t], recv_sem=recv_a.at[t], device_id=device, device_id_type=MESH)

    def spread(k):
        t, device = where(k)
        return pltpu.make_async_remote_copy(
            src_ref=out_ref.at[rows_of(me)], dst_ref=out_ref.at[rows_of(me)],
            send_sem=send_b.at[t], recv_sem=recv_b.at[me], device_id=device, device_id_type=MESH)

    def spreaded(k):
        t, device = where(k)
        return pltpu.make_async_remote_copy(
            src_ref=out_ref.at[rows_of(t)], dst_ref=out_ref.at[rows_of(t)],
            send_sem=send_b.at[t], recv_sem=recv_b.at[t], device_id=device, device_id_type=MESH)

    def loop(act):
        def body(k, _):
            act(k)
            return 0
        lax.fori_loop(1, total, body, 0)

    loop(lambda k: scatter(k).start())
    parts[me] = term_ref[rows_of(me), :]
    loop(lambda k: scattered(k).wait_recv())
    out_ref[rows_of(me), :] = jnp.sum(parts[...], axis=0)
    loop(lambda k: spread(k).start())
    loop(lambda k: spreaded(k).wait_recv())
    loop(lambda k: scattered(k).wait_send())
    loop(lambda k: spread(k).wait_send())


def invert_block(block):
    size = block.shape[0]
    row_id = lax.broadcasted_iota(jnp.int32, (size, size), 0)
    eye = row_id == lax.broadcasted_iota(jnp.int32, (size, size), 1)
    both = jnp.concatenate([block, eye.astype(jnp.float32)], axis=1)
    ids = lax.broadcasted_iota(jnp.int32, (size, 1), 0)
    for j in range(size - 1):
        row = both[j:j + 1, :] * (1.0 / both[j:j + 1, j:j + 1])
        column = jnp.where(ids > j, both[:, j:j + 1], 0.0)
        both = both - column * row
    pivot = jnp.sum(jnp.where(eye, both[:, :size], 0.0), axis=1, keepdims=True)
    return both[:, size:] / jnp.sqrt(pivot)


def factor_kernel(order, gram_ref, range_ref, total_ref, basis_ref, core_ref, work, inverse):
    rank = gram_ref.shape[0]
    nb = min(NB, rank)
    work[...] = gram_ref[...] / order
    ones = lax.broadcasted_iota(jnp.int32, (rank, rank), 0) == lax.broadcasted_iota(jnp.int32, (rank, rank), 1)
    inverse[...] = ones.astype(jnp.float32)
    for k in range(0, rank, nb):
        end = k + nb
        small = invert_block(work[k:end, k:end])
        line = nn(small, inverse[k:end, :], HIGHEST)
        inverse[k:end, :] = line
        if end < rank:
            panel = nt(work[end:, k:end], small, HIGHEST)
            work[end:, end:] = work[end:, end:] - nt(panel, panel, HIGHEST)
            inverse[end:, :] = inverse[end:, :] - nn(panel, line, HIGHEST)
    whole = inverse[...]
    basis_ref[...] = nt(range_ref[...], whole, HIGHEST)
    core_ref[...] = nt(nn(whole, total_ref[...], HIGHEST), whole, HIGHEST) / order


def fast(n, factor, gradient, sketch_ids):
    rows, cols = factor.shape
    rank = sketch_ids.shape[1]
    nz = n // 4
    per = cols // rows
    f32 = jnp.float32
    vmem = pl.BlockSpec(memory_space=pltpu.VMEM)
    shape = jax.ShapeDtypeStruct
    dma = pltpu.SemaphoreType.DMA
    factor_new, ranged, gram, term = pl.pallas_call(
        functools.partial(main_kernel, nz),
        out_shape=(shape((rows, cols), f32), shape((rows, rank), f32), shape((rank, rank), f32), shape((rank, rank), f32)),
        in_specs=[vmem, pl.BlockSpec(memory_space=pl.ANY), vmem],
        out_specs=(vmem, vmem, vmem, vmem),
        scratch_shapes=[
            pltpu.VMEM((n,) + gradient.shape, gradient.dtype),
            pltpu.VMEM((n, rows, gradient.shape[1]), gradient.dtype),
            pltpu.VMEM((2, rows, rank), f32),
            pltpu.VMEM((per, rows, rank), f32),
            pltpu.VMEM((2, rank, rank), f32),
            dma((4, n)), dma((n,)), dma((n,)), dma((n,)), dma((4, per)), dma((per,)), dma((2,)), dma((2,)), dma,
        ],
        compiler_params=pltpu.CompilerParams(collective_id=0, has_side_effects=True, vmem_limit_bytes=VMEM_BYTES),
    )(factor, gradient, sketch_ids)
    total = 2 * n
    summed = pl.pallas_call(
        functools.partial(sum_kernel, total),
        out_shape=shape((rank, rank), f32),
        in_specs=[vmem],
        out_specs=vmem,
        scratch_shapes=[
            pltpu.VMEM((total, rank // total, rank), f32),
            dma((total,)), dma((total,)), dma((total,)), dma((total,)),
        ],
        compiler_params=pltpu.CompilerParams(collective_id=1, has_side_effects=True),
    )(term)
    basis, core = pl.pallas_call(
        functools.partial(factor_kernel, rows * n),
        out_shape=(shape((rows, rank), f32), shape((rank, rank), f32)),
        in_specs=[vmem, vmem, vmem],
        out_specs=(vmem, vmem),
        scratch_shapes=[pltpu.VMEM((rank, rank), f32), pltpu.VMEM((rank, rank), f32)],
    )(gram, ranged, summed)
    return factor_new, basis, core


def from_root(block, axis, owner):
    block = jnp.where(lax.axis_index(axis) == owner, block, jnp.zeros_like(block))
    return lax.psum(block, axis)


def plain(n, factor, gradient, sketch_ids):
    rows_here, cols_here = factor.shape
    order = rows_here * n
    row_pos = lax.axis_index("row")
    fsdp_pos = lax.axis_index("fsdp")
    block_rows = lax.all_gather(gradient, "fsdp", axis=1, tiled=True)
    owner = fsdp_pos * rows_here // cols_here
    local_start = jnp.clip(fsdp_pos * rows_here - row_pos * cols_here, 0, cols_here - rows_here)
    own_slice = from_root(lax.dynamic_slice_in_dim(block_rows, local_start, rows_here, 0), "row", owner)
    factor_new = decay_rate * factor + nt(own_slice, block_rows)
    sketch = sketch_ids.astype(jnp.float32)
    ranged = lax.psum(jnp.dot(factor_new, sketch, precision=HIGHEST), "row")
    gram_matrix = lax.psum(jnp.dot(ranged.T, ranged, precision=HIGHEST), "fsdp") / order
    lower_factor = jnp.linalg.cholesky(gram_matrix)
    range_basis = jax.scipy.linalg.solve_triangular(lower_factor, ranged.T, lower=True).T
    gathered = lax.all_gather(range_basis, "fsdp", axis=0, tiled=True)
    picked = lax.dynamic_slice_in_dim(gathered, row_pos * cols_here, cols_here, 0)
    applied = jnp.dot(factor_new, picked, precision=HIGHEST)
    core_term = jnp.dot(range_basis.T, applied, precision=HIGHEST)
    return factor_new, range_basis, lax.psum(core_term, ("fsdp", "row")) / order


def solution(mesh):
    n, halves = mesh.shape["fsdp"], mesh.shape["row"]

    def shards(factor, gradient, sketch_ids):
        rows, cols = factor.shape
        rank = sketch_ids.shape[1]
        fits = (halves == 2 and n % 8 == 0 and n <= 16 and rows % 16 == 0 and cols % (4 * rows) == 0
                and rank % (16 * n) == 0 and rank % NB == 0)
        return (fast if fits else plain)(n, factor, gradient, sketch_ids)

    return jax.shard_map(
        shards,
        mesh=mesh,
        in_specs=(P("fsdp", "row"), P("row", "fsdp"), P("row", None)),
        out_specs=(P("fsdp", "row"), P("fsdp", None), P()),
        check_vma=False,
    )
```

time: 549 us -> 175 us (0.32)
  waiting for transfers between devices: 430 us -> 0 us
  Pallas kernels: 0 us -> 170 us
  other arithmetic: 61.7 us -> 0 us
  matrix products: 23.5 us -> 0 us
  between operations: 15.6 us -> 0.66 us
  local copies, waits for them, and re-layouts: 17.9 us -> 4.47 us
    psum x4 -> x0, waiting for transfers between devices: 295 us -> none  [the longest x1 124 us: shards(): projected_core = lax.psum(core_term, ('fsdp', 'row')) / B]
    pallas_call x0 -> x3, Pallas kernels: none -> 170 us  [the longest x1 123 us: fast(): pl.pallas_call(functools.partial(main_kernel, nz), out_shape=(shape((rows...]
    all_gather x2 -> x0, waiting for transfers between devices: 134 us -> none  [the longest x1 101 us: shards(): block_rows = lax.all_gather(gradient, 'fsdp', axis=1, tiled=True)]
    another operation x9 -> x0, other arithmetic: 53.7 us -> none  [the longest x6 34 us: shards(): lower_factor = jnp.linalg.cholesky(gram_matrix)]
    dot_general x5 -> x0, matrix products: 22.3 us -> none  [the longest x1 8.97 us: shards(): applied = jnp.dot(picked, gathered_piece, precision=highest)]
    gather x1 -> x0, local copies, waits for them, and re-layouts: 12.4 us -> none  [shards(): jnp.take(factor_new, jnp.clip(local_cols, 0, cols_here - 1), axis=1)]
  transfers between devices with their start and end apart: 6 -> 0, of which waited for: 6 -> 0; matrix products, arithmetic and copies ran while one was open for 2% -> 0% of each run, Pallas kernels for 0% -> 0%
where the time goes in v1:
time: 175 us
  Pallas kernels  170 us (97%)
  local copies, waits for them, and re-layouts  4.47 us (3%)
    pallas_call x1, Pallas kernels, fast(): pl.pallas_call(functools.partial(main_kernel, nz), out_shape=(shape((rows...  123 us
    pallas_call x1, Pallas kernels, fast(): pl.pallas_call(functools.partial(factor_kernel, rows * n), out_shape=(sha...  27 us
    pallas_call x1, Pallas kernels, fast(): pl.pallas_call(functools.partial(sum_kernel, total), out_shape=shape((ran...  19.8 us
    unnamed x10, local copies, waits for them, and re-layouts  4.47 us

profile of v1, /device:TPU:0, one launch (start us, length us, event | category | flops | bytes accessed | tf_op | source)
XLA Modules:
  0.0 174.7 jit_solution(17860573967428497519)
XLA Ops:
  0.6 1.4 copy.6.grad_ref
  2.0 122.9 %shard_map.58 = (f32[192,1536]{1,0:T(8,128)}, f32[192,256]{1,0:T(8,128)S(1)}, f32[256,256]{1,0:T(8,128)S(1)}, f32[256,256]{1,0:T(8,128)S(1)}) custom-call(f32[192,1536]{1,0:T(8,128)} %factor_ref.1, bf16[1536,240]{1,0:T(8,128)(2,1)S(1)} %copy.6.grad_ref, s32[1536,256]{1,0:T(8,128)} %sketch_ref.1), custom_call_target="tpu_custom_call" | custom-call | tf_op jit(solution)/shard_map/pallas_call | solution.py:310
  124.9 0.0 copy-start
  124.9 0.7 copy-done
  125.6 0.0 copy-start.1
  125.6 0.7 copy-done.1
  126.3 0.0 copy-start.2
  126.3 0.7 copy-done.2
  127.0 0.0 copy-start.3
  127.0 19.8 %shard_map.59.total_ref = f32[256,256]{1,0:T(8,128)} custom-call(f32[256,256]{1,0:T(8,128)} %copy-done), custom_call_target="tpu_custom_call" | custom-call | tf_op jit(solution)/shard_map/pallas_call | solution.py:326
  146.7 27.0 %shard_map.60 = (f32[192,256]{1,0:T(8,128)}, f32[256,256]{1,0:T(8,128)}) custom-call(f32[256,256]{1,0:T(8,128)} %copy-done.1, f32[192,256]{1,0:T(8,128)} %copy-done.2, f32[256,256]{1,0:T(8,128)} %shard_map.59.total_ref), custom_call_target="tpu_custom_call" | custom-call | tf_op jit(solution)/shard_map/pallas_call | solution.py:337
  173.7 0.0 copy-done.3
  173.7 1.0 copy.8
Async XLA Ops:
  124.9 0.7 copy-start
  125.6 0.7 copy-start.1
  126.3 0.7 copy-start.2
  127.0 46.7 %copy-start.3 = (f32[192,1536]{1,0:T(8,128)S(1)}, f32[192,1536]{1,0:T(8,128)}, u32[]{:S(2)}) copy-start(f32[192,1536]{1,0:T(8,128)} %get-tuple-element.18) | copy-start | bytes 3538948

commit v2 on v1

v2 whole, which is shorter than its diff:
```python
import functools

import jax
import jax.numpy as jnp
from jax import lax
from jax.experimental import pallas as pl
from jax.experimental.pallas import tpu as pltpu
from jax.sharding import PartitionSpec as P

decay_rate = 0.9
HIGHEST = lax.Precision.HIGHEST
MESH = pl.DeviceIdType.MESH
VMEM_BYTES = 52 * 1024 * 1024
NB = 64


def nt(a, b, precision=None):
    return lax.dot_general(a, b, (((1,), (1,)), ((), ())), precision=precision, preferred_element_type=jnp.float32)


def nn(a, b, precision=None):
    return lax.dot_general(a, b, (((1,), (0,)), ((), ())), precision=precision, preferred_element_type=jnp.float32)


def tn(a, b, precision=None):
    return lax.dot_general(a, b, (((0,), (0,)), ((), ())), precision=precision, preferred_element_type=jnp.float32)


def split(a):
    high = a.astype(jnp.bfloat16)
    return high, (a - high.astype(jnp.float32)).astype(jnp.bfloat16)


def place():
    f = lax.axis_index("fsdp")
    return f, lax.axis_index("row"), f // 4, (f // 2) % 2, f % 2


def relay(buf, slot, has, nz, send_sem, recv_sem, on_piece):
    f, x, z, y, c = place()

    def copy(piece, kind, target):
        return pltpu.make_async_remote_copy(
            src_ref=buf.at[slot(piece)], dst_ref=buf.at[slot(piece)],
            send_sem=send_sem.at[kind, slot(piece)], recv_sem=recv_sem.at[slot(piece)],
            device_id={"fsdp": target, "row": x}, device_id_type=MESH)

    def each(source, go, act):
        @pl.when(go)
        def _():
            piece = source * 4 + y * 2 + c

            @pl.when((source <= z) & (z + 1 < nz))
            def _():
                act(copy(piece, 0, f + 4))

            @pl.when((source >= z) & (z > 0))
            def _():
                act(copy(piece, 1, f - 4))

            act(copy(piece, 2, f + 2 - 4 * y))
            act(copy(piece, 3, f + 1 - 2 * c))

    def across(source, go, act):
        @pl.when(go)
        def _():
            act(copy(source * 4 + (1 - y) * 2 + c, 3, f + 1 - 2 * c))

    def at_distance(d):
        out = []
        for s in ([0] if d == 0 else [-d, d]):
            source = z + s
            ok = (source >= 0) & (source < nz)
            safe = jnp.clip(source, 0, nz - 1)
            out.append((safe, ok & has(safe)))
        return out

    def arrive(piece):
        copy(piece, 0, f + 1 - 2 * c).wait_recv()

    def serve(stage):
        own = at_distance(stage) if stage < nz else []
        far = at_distance(stage - 1) if stage > 0 else []
        for source, go in own:
            if stage > 0:
                @pl.when(go)
                def _(source=source):
                    arrive(source * 4 + y * 2 + c)
            each(source, go, lambda op: op.start())
        for source, go in far:
            @pl.when(go)
            def _(source=source):
                arrive(source * 4 + (1 - y) * 2 + c)
            across(source, go, lambda op: op.start())
        for sources, side in ((own, y), (far, 1 - y)):
            for source, go in sources:
                @pl.when(go)
                def _(source=source, side=side):
                    on_piece(source * 4 + side * 2 + c)
                    other = source * 4 + side * 2 + 1 - c
                    arrive(other)
                    on_piece(other)

    def finish():
        for stage in range(nz):
            for source, go in at_distance(stage):
                each(source, go, lambda op: op.wait_send())
                across(source, go, lambda op: op.wait_send())

    return serve, finish


def main_kernel(n, factor_ref, grad_ref, sketch_ref, new_ref, basis_ref, core_ref,
                grad_buf, own_buf, sketch_buf, sketch_own, thin_buf, part_buf, pass_buf, range_buf, own_range,
                gram_buf, term_buf, parts, total_buf, work, inverse,
                g_send, g_recv, o_send, o_recv, x_send, x_recv, r_send, r_recv,
                send_a, recv_a, send_b, recv_b, load_sem):
    f, x, z, y, c = place()
    nz = n // 4
    rows, cols = factor_ref.shape
    order = rows * n
    rank = sketch_ref.shape[1]
    per = cols // rows
    mine = (f // per) == x
    theirs = jnp.logical_not(mine)
    start = pl.multiple_of(jnp.clip(f - x * per, 0, per - 1) * rows, rows)
    own_rows = pl.ds(start, rows)
    load = pltpu.make_async_copy(grad_ref, grad_buf.at[f], load_sem)
    load.start()

    everyone = 2 * n
    me = 2 * f + x

    def where(k):
        t = lax.rem(me + k, everyone)
        return t, {"fsdp": t // 2, "row": lax.rem(t, 2)}

    def loop(act):
        def step(k, carry):
            act(k)
            return carry
        lax.fori_loop(1, everyone, step, 0)

    barrier = pltpu.get_barrier_semaphore()
    loop(lambda k: pl.semaphore_signal(barrier, inc=1, device_id=where(k)[1], device_id_type=MESH))
    pl.semaphore_wait(barrier, everyone - 1)

    def remote(src, dst, send, recv, target, row):
        return pltpu.make_async_remote_copy(
            src_ref=src, dst_ref=dst, send_sem=send, recv_sem=recv,
            device_id={"fsdp": target, "row": row}, device_id_type=MESH)

    def over_x(src, dst, k):
        return remote(src, dst, x_send.at[k], x_recv.at[k], f, 1 - x)

    def own_copy(piece):
        return remote(own_buf.at[piece], own_buf.at[piece], o_send.at[piece], o_recv.at[piece], f, 1 - x)

    load.wait()

    def on_grad(piece):
        @pl.when(mine)
        def _():
            own_buf[piece] = grad_buf[piece, own_rows, :]
            own_copy(piece).start()

        @pl.when(theirs)
        def _():
            own_copy(piece).wait_recv()

        new_ref[...] += nt(own_buf[piece], grad_buf[piece])

    serve, finish_grad = relay(grad_buf, lambda p: p, lambda s: s >= 0, nz, g_send, g_recv, on_grad)

    sketch = sketch_ref[...].astype(jnp.float32).astype(jnp.bfloat16)
    sketch_buf[...] = sketch
    give_sketch = over_x(sketch_own, sketch_own, 0)

    @pl.when(mine)
    def _():
        sketch_own[...] = sketch_buf[own_rows, :]
        give_sketch.start()

    thin_buf[0] = tn(grad_buf[f], sketch)
    trade_thin = over_x(thin_buf.at[0], thin_buf.at[1], 1)
    trade_thin.start()
    new_ref[...] = decay_rate * factor_ref[...]
    serve(0)

    @pl.when(theirs)
    def _():
        give_sketch.wait_recv()

    old_high, old_low = split(new_ref_scaled(factor_ref))
    own_sketch = sketch_own[...]
    old_part = tn(old_high, own_sketch) + tn(old_low, own_sketch)
    trade_thin.wait()
    thin_high, thin_low = split(thin_buf[0] + thin_buf[1])
    grad = grad_buf[f]
    part_buf[...] = old_part + nn(grad, thin_high) + nn(grad, thin_low)

    partners = (f + 1 - 2 * c, f + 2 - 4 * y, f + 4 - 8 * lax.rem(z, 2), f + 8 - 16 * (z // 2))
    bits = (c, y, lax.rem(z, 2), z // 2)
    base, size, used, steps = 0, cols, 0, []
    for partner, bit in zip(partners, bits):
        size = size // 2
        steps.append((partner, base + bit * size, base + (1 - bit) * size, size, used))
        base = base + bit * size
        used += size

    def span(at, size):
        return pl.ds(pl.multiple_of(at, 8), size)

    def reduce_copy(i):
        partner, keep, give, size, slot = steps[i]
        return remote(part_buf.at[span(give, size)], pass_buf.at[pl.ds(slot, size)], r_send.at[i], r_recv.at[i], partner, x)

    def reduce_end(i):
        partner, keep, give, size, slot = steps[i]
        reduce_copy(i).wait()
        part_buf[span(keep, size), :] += pass_buf[slot:slot + size, :]

    def gather_copy(i):
        partner, keep, give, size, slot = steps[i]
        return remote(range_buf.at[span(keep, size)], range_buf.at[span(keep, size)], r_send.at[4 + i], r_recv.at[4 + i], partner, x)

    reduce_copy(0).start()
    reduce_end(0)
    reduce_copy(1).start()
    serve(1)
    reduce_end(1)
    reduce_copy(2).start()
    reduce_end(2)
    reduce_copy(3).start()
    serve(2)
    reduce_end(3)
    last, size = steps[3][1], steps[3][3]
    range_buf[span(last, size), :] = part_buf[span(last, size), :]
    for i in (3, 2, 1, 0):
        gather_copy(i).start()
        if i == 1:
            serve(3)
        gather_copy(i).wait()

    give_range = over_x(own_range, own_range, 2)

    @pl.when(mine)
    def _():
        own_range[...] = range_buf[own_rows, :]
        give_range.start()

    meet_high, meet_low = split(range_buf[...])
    gram_buf[0] = tn(meet_high, meet_high) + tn(meet_high, meet_low) + tn(meet_low, meet_high)
    trade_gram = over_x(gram_buf.at[0], gram_buf.at[1], 3)
    trade_gram.start()
    thin_buf[2] = tn(grad_buf[f], meet_high) + tn(grad_buf[f], meet_low)
    trade_thin = over_x(thin_buf.at[2], thin_buf.at[3], 4)
    trade_thin.start()
    old_high, old_low = split(new_ref_scaled(factor_ref))
    applied_high, applied_low = split(nn(old_high, meet_high) + nn(old_low, meet_high) + nn(old_high, meet_low))

    @pl.when(theirs)
    def _():
        give_range.wait_recv()

    own_high, own_low = split(own_range[...])
    term = tn(own_high, applied_high) + tn(own_low, applied_high) + tn(own_high, applied_low)
    trade_gram.wait()
    trade_thin.wait()
    thin_high, thin_low = split(jnp.where(x == 0, thin_buf[2] + thin_buf[3], 0.0))
    term_buf[...] = term + tn(thin_high, thin_high) + tn(thin_high, thin_low) + tn(thin_low, thin_high)

    chunk = rank // everyone

    def rows_of(t):
        return pl.ds(pl.multiple_of(t * chunk, chunk), chunk)

    def scatter(k, slot):
        t, device = where(k)
        return pltpu.make_async_remote_copy(
            src_ref=term_buf.at[rows_of(t)], dst_ref=parts.at[me if slot is None else t],
            send_sem=send_a.at[t], recv_sem=recv_a.at[me if slot is None else t],
            device_id=device, device_id_type=MESH)

    def spread(k, slot):
        t, device = where(k)
        at = me if slot is None else t
        return pltpu.make_async_remote_copy(
            src_ref=total_buf.at[rows_of(at)], dst_ref=total_buf.at[rows_of(at)],
            send_sem=send_b.at[t], recv_sem=recv_b.at[at], device_id=device, device_id_type=MESH)

    loop(lambda k: scatter(k, None).start())
    parts[me] = term_buf[rows_of(me), :]
    work[...] = (gram_buf[0] + gram_buf[1]) / order
    ones = lax.broadcasted_iota(jnp.int32, (rank, rank), 0) == lax.broadcasted_iota(jnp.int32, (rank, rank), 1)
    inverse[...] = ones.astype(jnp.float32)
    eliminate(work, inverse, 0)
    eliminate(work, inverse, 1)
    loop(lambda k: scatter(k, 0).wait_recv())
    total_buf[rows_of(me), :] = jnp.sum(parts[...], axis=0)
    loop(lambda k: spread(k, None).start())
    for k in range(2, rank // NB):
        eliminate(work, inverse, k)
    whole = inverse[...]
    basis_ref[...] = nt(own_range[...], whole, HIGHEST)
    loop(lambda k: spread(k, 0).wait_recv())
    core_ref[...] = nt(nn(whole, total_buf[...], HIGHEST), whole, HIGHEST) / order

    serve(4)

    loop(lambda k: scatter(k, 0).wait_send())
    loop(lambda k: spread(k, None).wait_send())
    finish_grad()

    @pl.when(mine)
    def _():
        give_sketch.wait_send()
        give_range.wait_send()
        for piece in range(n):
            own_copy(piece).wait_send()


def new_ref_scaled(factor_ref):
    return decay_rate * factor_ref[...]


def invert_block(block):
    size = block.shape[0]
    row_id = lax.broadcasted_iota(jnp.int32, (size, size), 0)
    eye = row_id == lax.broadcasted_iota(jnp.int32, (size, size), 1)
    both = jnp.concatenate([block, eye.astype(jnp.float32)], axis=1)
    ids = lax.broadcasted_iota(jnp.int32, (size, 1), 0)
    for j in range(size - 1):
        row = both[j:j + 1, :] * (1.0 / both[j:j + 1, j:j + 1])
        column = jnp.where(ids > j, both[:, j:j + 1], 0.0)
        both = both - column * row
    pivot = jnp.sum(jnp.where(eye, both[:, :size], 0.0), axis=1, keepdims=True)
    return both[:, size:] / jnp.sqrt(pivot)


def eliminate(work, inverse, block):
    rank = work.shape[0]
    k, end = block * NB, (block + 1) * NB
    small = invert_block(work[k:end, k:end])
    line = nn(small, inverse[k:end, :], HIGHEST)
    inverse[k:end, :] = line
    if end < rank:
        panel = nt(work[end:, k:end], small, HIGHEST)
        work[end:, end:] = work[end:, end:] - nt(panel, panel, HIGHEST)
        inverse[end:, :] = inverse[end:, :] - nn(panel, line, HIGHEST)


def fast(n, factor, gradient, sketch_ids):
    rows, cols = factor.shape
    depth = gradient.shape[1]
    rank = sketch_ids.shape[1]
    f32, bf16 = jnp.float32, jnp.bfloat16
    vmem = pl.BlockSpec(memory_space=pltpu.VMEM)
    shape = jax.ShapeDtypeStruct
    dma = pltpu.SemaphoreType.DMA
    everyone = 2 * n
    return pl.pallas_call(
        functools.partial(main_kernel, n),
        out_shape=(shape((rows, cols), f32), shape((rows, rank), f32), shape((rank, rank), f32)),
        in_specs=[vmem, pl.BlockSpec(memory_space=pl.ANY), vmem],
        out_specs=(vmem, vmem, vmem),
        scratch_shapes=[
            pltpu.VMEM((n, cols, depth), bf16),
            pltpu.VMEM((n, rows, depth), bf16),
            pltpu.VMEM((cols, rank), bf16),
            pltpu.VMEM((rows, rank), bf16),
            pltpu.VMEM((4, depth, rank), f32),
            pltpu.VMEM((cols, rank), f32),
            pltpu.VMEM((cols, rank), f32),
            pltpu.VMEM((cols, rank), f32),
            pltpu.VMEM((rows, rank), f32),
            pltpu.VMEM((2, rank, rank), f32),
            pltpu.VMEM((rank, rank), f32),
            pltpu.VMEM((everyone, rank // everyone, rank), f32),
            pltpu.VMEM((rank, rank), f32),
            pltpu.VMEM((rank, rank), f32),
            pltpu.VMEM((rank, rank), f32),
            dma((4, n)), dma((n,)), dma((n,)), dma((n,)), dma((5,)), dma((5,)), dma((8,)), dma((8,)),
            dma((everyone,)), dma((everyone,)), dma((everyone,)), dma((everyone,)), dma,
        ],
        compiler_params=pltpu.CompilerParams(collective_id=0, has_side_effects=True, vmem_limit_bytes=VMEM_BYTES),
    )(factor, gradient, sketch_ids)


def from_root(block, axis, owner):
    block = jnp.where(lax.axis_index(axis) == owner, block, jnp.zeros_like(block))
    return lax.psum(block, axis)


def plain(n, factor, gradient, sketch_ids):
    rows_here, cols_here = factor.shape
    order = rows_here * n
    row_pos = lax.axis_index("row")
    fsdp_pos = lax.axis_index("fsdp")
    block_rows = lax.all_gather(gradient, "fsdp", axis=1, tiled=True)
    owner = fsdp_pos * rows_here // cols_here
    local_start = jnp.clip(fsdp_pos * rows_here - row_pos * cols_here, 0, cols_here - rows_here)
    own_slice = from_root(lax.dynamic_slice_in_dim(block_rows, local_start, rows_here, 0), "row", owner)
    factor_new = decay_rate * factor + nt(own_slice, block_rows)
    sketch = sketch_ids.astype(jnp.float32)
    ranged = lax.psum(jnp.dot(factor_new, sketch, precision=HIGHEST), "row")
    gram_matrix = lax.psum(jnp.dot(ranged.T, ranged, precision=HIGHEST), "fsdp") / order
    lower_factor = jnp.linalg.cholesky(gram_matrix)
    range_basis = jax.scipy.linalg.solve_triangular(lower_factor, ranged.T, lower=True).T
    gathered = lax.all_gather(range_basis, "fsdp", axis=0, tiled=True)
    picked = lax.dynamic_slice_in_dim(gathered, row_pos * cols_here, cols_here, 0)
    applied = jnp.dot(factor_new, picked, precision=HIGHEST)
    core_term = jnp.dot(range_basis.T, applied, precision=HIGHEST)
    return factor_new, range_basis, lax.psum(core_term, ("fsdp", "row")) / order


def solution(mesh):
    n, halves = mesh.shape["fsdp"], mesh.shape["row"]

    def shards(factor, gradient, sketch_ids):
        rows, cols = factor.shape
        rank = sketch_ids.shape[1]
        fits = (halves == 2 and n == 16 and rows % 16 == 0 and cols == 8 * rows
                and rank % (16 * n) == 0 and rank % NB == 0)
        return (fast if fits else plain)(n, factor, gradient, sketch_ids)

    return jax.shard_map(
        shards,
        mesh=mesh,
        in_specs=(P("fsdp", "row"), P("row", "fsdp"), P("row", None)),
        out_specs=(P("fsdp", "row"), P("fsdp", None), P()),
        check_vma=False,
    )
```

time: 175 us -> 163 us (0.931)
  Pallas kernels: 170 us -> 156 us
    pallas_call x3 -> x1, Pallas kernels: 170 us -> 156 us  [fast(): pl.pallas_call(functools.partial(main_kernel, n), out_shape=(shape((rows,...]
    unnamed x10 -> x4, local copies, waits for them, and re-layouts: 4.47 us -> 5.12 us
where the time goes in v2:
time: 163 us; the launch traced here: 162 us
  Pallas kernels  156 us (96%)
  local copies, waits for them, and re-layouts  5.12 us (3%)
    pallas_call x1, Pallas kernels, fast(): pl.pallas_call(functools.partial(main_kernel, n), out_shape=(shape((rows,...  156 us
    unnamed x4, local copies, waits for them, and re-layouts  5.12 us

profile of v2, /device:TPU:0, one launch (start us, length us, event | category | flops | bytes accessed | tf_op | source)
XLA Modules:
  0.0 161.9 jit_solution(11101439468457710188)
XLA Ops:
  0.6 1.4 copy.6.grad_ref
  2.0 156.2 %shard_map.58 = (f32[192,1536]{1,0:T(8,128)}, f32[192,256]{1,0:T(8,128)S(1)}, f32[256,256]{1,0:T(8,128)S(1)}) custom-call(f32[192,1536]{1,0:T(8,128)} %factor_ref.1, bf16[1536,240]{1,0:T(8,128)(2,1)S(1)} %copy.6.grad_ref, s32[1536,256]{1,0:T(8,128)} %sketch_ref.1), custom_call_target="tpu_custom_call" | custom-call | tf_op jit(solution)/shard_map/pallas_call | solution.py:362
  158.2 2.4 %copy.10 = f32[192,1536]{1,0:T(8,128)} copy(f32[192,1536]{1,0:T(8,128)} %get-tuple-element.6) | data formatting | bytes 2359296
  160.6 0.7 copy.11
  161.2 0.7 copy.12

commit v3 on v2

--- a/solution.py
+++ b/solution.py
@@ -36,88 +36,15 @@
     return f, lax.axis_index("row"), f // 4, (f // 2) % 2, f % 2
 
 
-def relay(buf, slot, has, nz, send_sem, recv_sem, on_piece):
-    f, x, z, y, c = place()
-
-    def copy(piece, kind, target):
-        return pltpu.make_async_remote_copy(
-            src_ref=buf.at[slot(piece)], dst_ref=buf.at[slot(piece)],
-            send_sem=send_sem.at[kind, slot(piece)], recv_sem=recv_sem.at[slot(piece)],
-            device_id={"fsdp": target, "row": x}, device_id_type=MESH)
-
-    def each(source, go, act):
-        @pl.when(go)
-        def _():
-            piece = source * 4 + y * 2 + c
-
-            @pl.when((source <= z) & (z + 1 < nz))
-            def _():
-                act(copy(piece, 0, f + 4))
-
-            @pl.when((source >= z) & (z > 0))
-            def _():
-                act(copy(piece, 1, f - 4))
-
-            act(copy(piece, 2, f + 2 - 4 * y))
-            act(copy(piece, 3, f + 1 - 2 * c))
-
-    def across(source, go, act):
-        @pl.when(go)
-        def _():
-            act(copy(source * 4 + (1 - y) * 2 + c, 3, f + 1 - 2 * c))
-
-    def at_distance(d):
-        out = []
-        for s in ([0] if d == 0 else [-d, d]):
-            source = z + s
-            ok = (source >= 0) & (source < nz)
-            safe = jnp.clip(source, 0, nz - 1)
-            out.append((safe, ok & has(safe)))
-        return out
-
-    def arrive(piece):
-        copy(piece, 0, f + 1 - 2 * c).wait_recv()
-
-    def serve(stage):
-        own = at_distance(stage) if stage < nz else []
-        far = at_distance(stage - 1) if stage > 0 else []
-        for source, go in own:
-            if stage > 0:
-                @pl.when(go)
-                def _(source=source):
-                    arrive(source * 4 + y * 2 + c)
-            each(source, go, lambda op: op.start())
-        for source, go in far:
-            @pl.when(go)
-            def _(source=source):
-                arrive(source * 4 + (1 - y) * 2 + c)
-            across(source, go, lambda op: op.start())
-        for sources, side in ((own, y), (far, 1 - y)):
-            for source, go in sources:
-                @pl.when(go)
-                def _(source=source, side=side):
-                    on_piece(source * 4 + side * 2 + c)
-                    other = source * 4 + side * 2 + 1 - c
-                    arrive(other)
-                    on_piece(other)
-
-    def finish():
-        for stage in range(nz):
-            for source, go in at_distance(stage):
-                each(source, go, lambda op: op.wait_send())
-                across(source, go, lambda op: op.wait_send())
-
-    return serve, finish
-
-
 def main_kernel(n, factor_ref, grad_ref, sketch_ref, new_ref, basis_ref, core_ref,
                 grad_buf, own_buf, sketch_buf, sketch_own, thin_buf, part_buf, pass_buf, range_buf, own_range,
-                gram_buf, term_buf, parts, total_buf, work, inverse,
-                g_send, g_recv, o_send, o_recv, x_send, x_recv, r_send, r_recv,
+                gram_buf, term_buf, parts, total_buf, work, inverse, core_give, core_take, y_give, y_take,
+                g_send, g_recv, o_send, o_recv, x_send, x_recv, r_send, r_recv, z_send, z_recv, c_send, c_recv, y_send, y_recv,
                 send_a, recv_a, send_b, recv_b, load_sem):
     f, x, z, y, c = place()
     nz = n // 4
     rows, cols = factor_ref.shape
+    half, depth = grad_buf.shape[2:]
     order = rows * n
     rank = sketch_ref.shape[1]
     per = cols // rows
@@ -125,8 +52,13 @@
     theirs = jnp.logical_not(mine)
     start = pl.multiple_of(jnp.clip(f - x * per, 0, per - 1) * rows, rows)
     own_rows = pl.ds(start, rows)
-    load = pltpu.make_async_copy(grad_ref, grad_buf.at[f], load_sem)
-    load.start()
+    own_half = lax.rem(z, 2)
+
+    def load(h):
+        return pltpu.make_async_copy(grad_ref.at[pl.ds(h * half, half)], grad_buf.at[z, h], load_sem.at[h])
+
+    load(0).start()
+    load(1).start()
 
     everyone = 2 * n
     me = 2 * f + x
@@ -153,24 +85,39 @@
     def over_x(src, dst, k):
         return remote(src, dst, x_send.at[k], x_recv.at[k], f, 1 - x)
 
-    def own_copy(piece):
-        return remote(own_buf.at[piece], own_buf.at[piece], o_send.at[piece], o_recv.at[piece], f, 1 - x)
-
-    load.wait()
-
-    def on_grad(piece):
-        @pl.when(mine)
+    load(0).wait()
+    load(1).wait()
+
+    def hop(source, h, kind, target):
+        return remote(grad_buf.at[source, h], grad_buf.at[source, h],
+                      g_send.at[kind, 2 * source + h], g_recv.at[2 * source + h], target, x)
+
+    def own_copy(source):
+        return remote(grad_buf.at[source, own_half], own_buf.at[source], o_send.at[source], o_recv.at[source], f, 1 - x)
+
+    def pass_on(source, h, act):
+        @pl.when((source <= z) & (z + 1 < nz))
         def _():
-            own_buf[piece] = grad_buf[piece, own_rows, :]
-            own_copy(piece).start()
-
-        @pl.when(theirs)
+            act(hop(source, h, 0, f + 4))
+
+        @pl.when((source >= z) & (z > 0))
         def _():
-            own_copy(piece).wait_recv()
-
-        new_ref[...] += nt(own_buf[piece], grad_buf[piece])
-
-    serve, finish_grad = relay(grad_buf, lambda p: p, lambda s: s >= 0, nz, g_send, g_recv, on_grad)
+            act(hop(source, h, 1, f - 4))
+
+    def serve(stage, h):
+        for shift in ([0] if stage == 0 else [-stage, stage]):
+            source = jnp.clip(z + shift, 0, nz - 1)
+
+            @pl.when((z + shift >= 0) & (z + shift < nz))
+            def _(source=source):
+                if stage > 0:
+                    hop(source, h, 0, f + 1 - 2 * c).wait_recv()
+                pass_on(source, h, lambda op: op.start())
+
+                @pl.when(mine & (own_half == h))
+                def _():
+                    own_copy(source).start()
+                    own_buf[source] = grad_buf[source, h]
 
     sketch = sketch_ref[...].astype(jnp.float32).astype(jnp.bfloat16)
     sketch_buf[...] = sketch
@@ -181,11 +128,12 @@
         sketch_own[...] = sketch_buf[own_rows, :]
         give_sketch.start()
 
-    thin_buf[0] = tn(grad_buf[f], sketch)
+    grad = grad_buf[z].reshape(cols, depth)
+    thin_buf[0] = tn(grad, sketch)
     trade_thin = over_x(thin_buf.at[0], thin_buf.at[1], 1)
     trade_thin.start()
-    new_ref[...] = decay_rate * factor_ref[...]
-    serve(0)
+    serve(0, 0)
+    serve(0, 1)
 
     @pl.when(theirs)
     def _():
@@ -193,23 +141,19 @@
 
     old_high, old_low = split(new_ref_scaled(factor_ref))
     own_sketch = sketch_own[...]
-    old_part = tn(old_high, own_sketch) + tn(old_low, own_sketch)
+    part_buf[...] = tn(old_high, own_sketch) + tn(old_low, own_sketch)
     trade_thin.wait()
     thin_high, thin_low = split(thin_buf[0] + thin_buf[1])
-    grad = grad_buf[f]
-    part_buf[...] = old_part + nn(grad, thin_high) + nn(grad, thin_low)
-
-    partners = (f + 1 - 2 * c, f + 2 - 4 * y, f + 4 - 8 * lax.rem(z, 2), f + 8 - 16 * (z // 2))
-    bits = (c, y, lax.rem(z, 2), z // 2)
-    base, size, used, steps = 0, cols, 0, []
-    for partner, bit in zip(partners, bits):
-        size = size // 2
-        steps.append((partner, base + bit * size, base + (1 - bit) * size, size, used))
-        base = base + bit * size
-        used += size
+    part_buf[...] += nn(grad, thin_high) + nn(grad, thin_low)
 
     def span(at, size):
         return pl.ds(pl.multiple_of(at, 8), size)
+
+    sibling, across = f + 1 - 2 * c, f + 2 - 4 * y
+    quarter = cols // 4
+    small = quarter // nz
+    at_y = c * half + y * quarter
+    steps = ((sibling, c * half, (1 - c) * half, half, 0), (across, at_y, c * half + (1 - y) * quarter, quarter, half))
 
     def reduce_copy(i):
         partner, keep, give, size, slot = steps[i]
@@ -222,25 +166,48 @@
 
     def gather_copy(i):
         partner, keep, give, size, slot = steps[i]
-        return remote(range_buf.at[span(keep, size)], range_buf.at[span(keep, size)], r_send.at[4 + i], r_recv.at[4 + i], partner, x)
-
+        return remote(range_buf.at[span(keep, size)], range_buf.at[span(keep, size)], r_send.at[2 + i], r_recv.at[2 + i], partner, x)
+
+    def line(k):
+        t = lax.rem(z + k, nz)
+        return t, f + 4 * (t - z)
+
+    def line_reduce(k, sending):
+        t, target = line(k)
+        slot = half + quarter + (z if sending else t) * small
+        return remote(part_buf.at[span(at_y + t * small, small)], pass_buf.at[span(slot, small)],
+                      z_send.at[0, t], z_recv.at[0, z if sending else t], target, x)
+
+    def line_gather(k, sending):
+        t, target = line(k)
+        here = span(at_y + (z if sending else t) * small, small)
+        return remote(range_buf.at[here], range_buf.at[here],
+                      z_send.at[1, t], z_recv.at[1, z if sending else t], target, x)
+
+    peers = range(1, nz)
     reduce_copy(0).start()
     reduce_end(0)
     reduce_copy(1).start()
-    serve(1)
+    serve(1, 0)
     reduce_end(1)
-    reduce_copy(2).start()
-    reduce_end(2)
-    reduce_copy(3).start()
-    serve(2)
-    reduce_end(3)
-    last, size = steps[3][1], steps[3][3]
-    range_buf[span(last, size), :] = part_buf[span(last, size), :]
-    for i in (3, 2, 1, 0):
-        gather_copy(i).start()
-        if i == 1:
-            serve(3)
-        gather_copy(i).wait()
+    for k in peers:
+        line_reduce(k, True).start()
+    serve(1, 1)
+    total = part_buf[span(at_y + z * small, small), :]
+    for k in peers:
+        line_reduce(k, False).wait_recv()
+        total = total + pass_buf[span(half + quarter + line(k)[0] * small, small), :]
+    range_buf[span(at_y + z * small, small), :] = total
+    for k in peers:
+        line_gather(k, True).start()
+    serve(2, 0)
+    for k in peers:
+        line_gather(k, False).wait_recv()
+    gather_copy(1).start()
+    serve(2, 1)
+    gather_copy(1).wait()
+    gather_copy(0).start()
+    gather_copy(0).wait()
 
     give_range = over_x(own_range, own_range, 2)
 
@@ -253,7 +220,7 @@
     gram_buf[0] = tn(meet_high, meet_high) + tn(meet_high, meet_low) + tn(meet_low, meet_high)
     trade_gram = over_x(gram_buf.at[0], gram_buf.at[1], 3)
     trade_gram.start()
-    thin_buf[2] = tn(grad_buf[f], meet_high) + tn(grad_buf[f], meet_low)
+    thin_buf[2] = tn(grad, meet_high) + tn(grad, meet_low)
     trade_thin = over_x(thin_buf.at[2], thin_buf.at[3], 4)
     trade_thin.start()
     old_high, old_low = split(new_ref_scaled(factor_ref))
@@ -294,30 +261,81 @@
     work[...] = (gram_buf[0] + gram_buf[1]) / order
     ones = lax.broadcasted_iota(jnp.int32, (rank, rank), 0) == lax.broadcasted_iota(jnp.int32, (rank, rank), 1)
     inverse[...] = ones.astype(jnp.float32)
+
+    def block(side, core, h):
+        at = pl.ds(pl.multiple_of((2 * side + core) * rows, rows), rows)
+        out = nt(own_buf[0, at, :], grad_buf[0, h])
+        for source in range(1, nz):
+            out = out + nt(own_buf[source, at, :], grad_buf[source, h])
+        return out
+
+    def core_copy(h):
+        return remote(core_give.at[h], core_take.at[h], c_send.at[h], c_recv.at[h], sibling, x)
+
+    def y_copy(h):
+        return remote(y_give.at[h], y_take.at[h], y_send.at[h], y_recv.at[h], across, x)
+
+    def first(h):
+        for side in range(2):
+            core_give[h, side] = block(side, 1 - c, h)
+        core_copy(h).start()
+        y_give[h] = block(1 - y, c, h)
+        here = slice(h * half, (h + 1) * half)
+        new_ref[:, here] = decay_rate * factor_ref[:, here] + block(y, c, h)
+
+    def second(h):
+        core_copy(h).wait_recv()
+        y_give[h] += core_take[h, 1 - y]
+        y_copy(h).start()
+        new_ref[:, h * half:(h + 1) * half] += core_take[h, y]
+
+    def third(h):
+        y_copy(h).wait_recv()
+        new_ref[:, h * half:(h + 1) * half] += y_take[h]
+
+    serve(3, 0)
+    serve(3, 1)
+
+    @pl.when(theirs)
+    def _():
+        for source in range(nz):
+            own_copy(source).wait_recv()
+
+    first(0)
+    first(1)
     eliminate(work, inverse, 0)
+    second(0)
+    second(1)
     eliminate(work, inverse, 1)
     loop(lambda k: scatter(k, 0).wait_recv())
     total_buf[rows_of(me), :] = jnp.sum(parts[...], axis=0)
     loop(lambda k: spread(k, None).start())
     for k in range(2, rank // NB):
         eliminate(work, inverse, k)
+    third(0)
+    third(1)
     whole = inverse[...]
     basis_ref[...] = nt(own_range[...], whole, HIGHEST)
     loop(lambda k: spread(k, 0).wait_recv())
     core_ref[...] = nt(nn(whole, total_buf[...], HIGHEST), whole, HIGHEST) / order
 
-    serve(4)
-
     loop(lambda k: scatter(k, 0).wait_send())
     loop(lambda k: spread(k, None).wait_send())
-    finish_grad()
+    for h in range(2):
+        core_copy(h).wait_send()
+        y_copy(h).wait_send()
+        for source in range(nz):
+            pass_on(source, h, lambda op: op.wait_send())
+    for k in peers:
+        line_reduce(k, True).wait_send()
+        line_gather(k, True).wait_send()
 
     @pl.when(mine)
     def _():
         give_sketch.wait_send()
         give_range.wait_send()
-        for piece in range(n):
-            own_copy(piece).wait_send()
+        for source in range(nz):
+            own_copy(source).wait_send()
 
 
 def new_ref_scaled(factor_ref):
@@ -358,15 +376,15 @@
     vmem = pl.BlockSpec(memory_space=pltpu.VMEM)
     shape = jax.ShapeDtypeStruct
     dma = pltpu.SemaphoreType.DMA
-    everyone = 2 * n
+    everyone, nz, half = 2 * n, n // 4, cols // 2
     return pl.pallas_call(
         functools.partial(main_kernel, n),
         out_shape=(shape((rows, cols), f32), shape((rows, rank), f32), shape((rank, rank), f32)),
         in_specs=[vmem, pl.BlockSpec(memory_space=pl.ANY), vmem],
         out_specs=(vmem, vmem, vmem),
         scratch_shapes=[
-            pltpu.VMEM((n, cols, depth), bf16),
-            pltpu.VMEM((n, rows, depth), bf16),
+            pltpu.VMEM((nz, 2, half, depth), bf16),
+            pltpu.VMEM((nz, half, depth), bf16),
             pltpu.VMEM((cols, rank), bf16),
             pltpu.VMEM((rows, rank), bf16),
             pltpu.VMEM((4, depth, rank), f32),
@@ -380,8 +398,13 @@
             pltpu.VMEM((rank, rank), f32),
             pltpu.VMEM((rank, rank), f32),
             pltpu.VMEM((rank, rank), f32),
-            dma((4, n)), dma((n,)), dma((n,)), dma((n,)), dma((5,)), dma((5,)), dma((8,)), dma((8,)),
-            dma((everyone,)), dma((everyone,)), dma((everyone,)), dma((everyone,)), dma,
+            pltpu.VMEM((2, 2, rows, half), f32),
+            pltpu.VMEM((2, 2, rows, half), f32),
+            pltpu.VMEM((2, rows, half), f32),
+            pltpu.VMEM((2, rows, half), f32),
+            dma((2, 2 * nz)), dma((2 * nz,)), dma((nz,)), dma((nz,)), dma((5,)), dma((5,)), dma((4,)), dma((4,)),
+            dma((2, nz)), dma((2, nz)), dma((2,)), dma((2,)), dma((2,)), dma((2,)),
+            dma((everyone,)), dma((everyone,)), dma((everyone,)), dma((everyone,)), dma((2,)),
         ],
         compiler_params=pltpu.CompilerParams(collective_id=0, has_side_effects=True, vmem_limit_bytes=VMEM_BYTES),
     )(factor, gradient, sketch_ids)
@@ -420,7 +443,7 @@
     def shards(factor, gradient, sketch_ids):
         rows, cols = factor.shape
         rank = sketch_ids.shape[1]
-        fits = (halves == 2 and n == 16 and rows % 16 == 0 and cols == 8 * rows
+        fits = (halves == 2 and n == 16 and rows % 64 == 0 and cols == 8 * rows
                 and rank % (16 * n) == 0 and rank % NB == 0)
         return (fast if fits else plain)(n, factor, gradient, sketch_ids)
 

time: 163 us -> 149 us (0.914)
  the two profiles are of different devices: /device:TPU:0 before, /device:TPU:24 now
where the time goes in v3:
time: 149 us
  Pallas kernels  143 us (96%)
  local copies, waits for them, and re-layouts  5.12 us (3%)
    pallas_call x1, Pallas kernels, fast(): pl.pallas_call(functools.partial(main_kernel, n), out_shape=(shape((rows,...  143 us
    unnamed x4, local copies, waits for them, and re-layouts  5.12 us

profile of v3, /device:TPU:24, one launch (start us, length us, event | category | flops | bytes accessed | tf_op | source)
XLA Modules:
  0.0 148.8 jit_solution(9298471333685394952)
XLA Ops:
  0.6 1.4 copy.6.grad_ref
  2.0 143.0 %shard_map.58 = (f32[192,1536]{1,0:T(8,128)}, f32[192,256]{1,0:T(8,128)S(1)}, f32[256,256]{1,0:T(8,128)S(1)}) custom-call(f32[192,1536]{1,0:T(8,128)} %factor_ref.1, bf16[1536,240]{1,0:T(8,128)(2,1)S(1)} %copy.6.grad_ref, s32[1536,256]{1,0:T(8,128)} %sketch_ref.1), custom_call_target="tpu_custom_call" | custom-call | tf_op jit(solution)/shard_map/pallas_call | solution.py:380
  145.1 2.4 %copy.10 = f32[192,1536]{1,0:T(8,128)} copy(f32[192,1536]{1,0:T(8,128)} %get-tuple-element.6) | data formatting | bytes 2359296
  147.4 0.7 copy.11
  148.1 0.7 copy.12

commit v4 on v3

--- a/solution.py
+++ b/solution.py
@@ -40,7 +40,7 @@
                 grad_buf, own_buf, sketch_buf, sketch_own, thin_buf, part_buf, pass_buf, range_buf, own_range,
                 gram_buf, term_buf, parts, total_buf, work, inverse, core_give, core_take, y_give, y_take,
                 g_send, g_recv, o_send, o_recv, x_send, x_recv, r_send, r_recv, z_send, z_recv, c_send, c_recv, y_send, y_recv,
-                send_a, recv_a, send_b, recv_b, load_sem):
+                s_send, s_recv, load_sem):
     f, x, z, y, c = place()
     nz = n // 4
     rows, cols = factor_ref.shape
@@ -60,22 +60,17 @@
     load(0).start()
     load(1).start()
 
-    everyone = 2 * n
-    me = 2 * f + x
-
-    def where(k):
-        t = lax.rem(me + k, everyone)
-        return t, {"fsdp": t // 2, "row": lax.rem(t, 2)}
-
-    def loop(act):
-        def step(k, carry):
-            act(k)
-            return carry
-        lax.fori_loop(1, everyone, step, 0)
+    sibling, across = f + 1 - 2 * c, f + 2 - 4 * y
+    peers = range(1, nz)
+
+    def line(k):
+        t = lax.rem(z + k, nz)
+        return t, f + 4 * (t - z)
 
     barrier = pltpu.get_barrier_semaphore()
-    loop(lambda k: pl.semaphore_signal(barrier, inc=1, device_id=where(k)[1], device_id_type=MESH))
-    pl.semaphore_wait(barrier, everyone - 1)
+    for target, row in [(f, 1 - x), (sibling, x), (across, x)] + [(line(k)[1], x) for k in peers]:
+        pl.semaphore_signal(barrier, inc=1, device_id={"fsdp": target, "row": row}, device_id_type=MESH)
+    pl.semaphore_wait(barrier, nz + 2)
 
     def remote(src, dst, send, recv, target, row):
         return pltpu.make_async_remote_copy(
@@ -149,7 +144,6 @@
     def span(at, size):
         return pl.ds(pl.multiple_of(at, 8), size)
 
-    sibling, across = f + 1 - 2 * c, f + 2 - 4 * y
     quarter = cols // 4
     small = quarter // nz
     at_y = c * half + y * quarter
@@ -167,10 +161,6 @@
     def gather_copy(i):
         partner, keep, give, size, slot = steps[i]
         return remote(range_buf.at[span(keep, size)], range_buf.at[span(keep, size)], r_send.at[2 + i], r_recv.at[2 + i], partner, x)
-
-    def line(k):
-        t = lax.rem(z + k, nz)
-        return t, f + 4 * (t - z)
 
     def line_reduce(k, sending):
         t, target = line(k)
@@ -184,15 +174,14 @@
         return remote(range_buf.at[here], range_buf.at[here],
                       z_send.at[1, t], z_recv.at[1, z if sending else t], target, x)
 
-    peers = range(1, nz)
     reduce_copy(0).start()
     reduce_end(0)
     reduce_copy(1).start()
     serve(1, 0)
+    serve(1, 1)
     reduce_end(1)
     for k in peers:
         line_reduce(k, True).start()
-    serve(1, 1)
     total = part_buf[span(at_y + z * small, small), :]
     for k in peers:
         line_reduce(k, False).wait_recv()
@@ -201,14 +190,25 @@
     for k in peers:
         line_gather(k, True).start()
     serve(2, 0)
+    serve(2, 1)
     for k in peers:
         line_gather(k, False).wait_recv()
     gather_copy(1).start()
-    serve(2, 1)
     gather_copy(1).wait()
     gather_copy(0).start()
     gather_copy(0).wait()
 
+    def side_rows(i, count):
+        return pl.ds(pl.multiple_of(i * count, 8), count)
+
+    meet_high, meet_low = split(range_buf[...])
+    gram_buf[0] = tn(meet_high, meet_high) + tn(meet_high, meet_low) + tn(meet_low, meet_high)
+    part = rank // 2
+    trade_gram = over_x(gram_buf.at[0, side_rows(c, part)], gram_buf.at[1, side_rows(c, part)], 3)
+    trade_gram.start()
+    thin_buf[2] = tn(grad, meet_high) + tn(grad, meet_low)
+    trade_thin = over_x(thin_buf.at[2], thin_buf.at[3], 4)
+    trade_thin.start()
     give_range = over_x(own_range, own_range, 2)
 
     @pl.when(mine)
@@ -216,51 +216,44 @@
         own_range[...] = range_buf[own_rows, :]
         give_range.start()
 
-    meet_high, meet_low = split(range_buf[...])
-    gram_buf[0] = tn(meet_high, meet_high) + tn(meet_high, meet_low) + tn(meet_low, meet_high)
-    trade_gram = over_x(gram_buf.at[0], gram_buf.at[1], 3)
-    trade_gram.start()
-    thin_buf[2] = tn(grad, meet_high) + tn(grad, meet_low)
-    trade_thin = over_x(thin_buf.at[2], thin_buf.at[3], 4)
-    trade_thin.start()
-    old_high, old_low = split(new_ref_scaled(factor_ref))
-    applied_high, applied_low = split(nn(old_high, meet_high) + nn(old_low, meet_high) + nn(old_high, meet_low))
-
-    @pl.when(theirs)
-    def _():
-        give_range.wait_recv()
-
-    own_high, own_low = split(own_range[...])
-    term = tn(own_high, applied_high) + tn(own_low, applied_high) + tn(own_high, applied_low)
-    trade_gram.wait()
-    trade_thin.wait()
-    thin_high, thin_low = split(jnp.where(x == 0, thin_buf[2] + thin_buf[3], 0.0))
-    term_buf[...] = term + tn(thin_high, thin_high) + tn(thin_high, thin_low) + tn(thin_low, thin_high)
-
-    chunk = rank // everyone
-
-    def rows_of(t):
-        return pl.ds(pl.multiple_of(t * chunk, chunk), chunk)
-
-    def scatter(k, slot):
-        t, device = where(k)
-        return pltpu.make_async_remote_copy(
-            src_ref=term_buf.at[rows_of(t)], dst_ref=parts.at[me if slot is None else t],
-            send_sem=send_a.at[t], recv_sem=recv_a.at[me if slot is None else t],
-            device_id=device, device_id_type=MESH)
-
-    def spread(k, slot):
-        t, device = where(k)
-        at = me if slot is None else t
-        return pltpu.make_async_remote_copy(
-            src_ref=total_buf.at[rows_of(at)], dst_ref=total_buf.at[rows_of(at)],
-            send_sem=send_b.at[t], recv_sem=recv_b.at[at], device_id=device, device_id_type=MESH)
-
-    loop(lambda k: scatter(k, None).start())
-    parts[me] = term_buf[rows_of(me), :]
-    work[...] = (gram_buf[0] + gram_buf[1]) / order
-    ones = lax.broadcasted_iota(jnp.int32, (rank, rank), 0) == lax.broadcasted_iota(jnp.int32, (rank, rank), 1)
-    inverse[...] = ones.astype(jnp.float32)
+    def hand(i, src, dst, target, row):
+        return remote(src, dst, s_send.at[i], s_recv.at[i], target, row)
+
+    both, four, fine = rank // 2, rank // 4, rank // (4 * nz)
+    four_at = c * both + y * four
+
+    def sum_core():
+        return hand(0, term_buf.at[side_rows(1 - c, both)], parts.at[pl.ds(0, both)], sibling, x)
+
+    def sum_y():
+        return hand(1, term_buf.at[span(c * both + (1 - y) * four, four)], parts.at[pl.ds(both, four)], across, x)
+
+    def sum_x():
+        return hand(2, term_buf.at[span(four_at, four)], parts.at[pl.ds(both + four, four)], f, 1 - x)
+
+    def sum_z(k, sending):
+        t, target = line(k)
+        at = z if sending else t
+        return remote(term_buf.at[span(four_at + t * fine, fine)], parts.at[span(both + 2 * four + at * fine, fine)],
+                      z_send.at[2, t], z_recv.at[2, at], target, x)
+
+    def back_z(k, sending):
+        t, target = line(k)
+        at = z if sending else t
+        here = span(four_at + at * fine, fine)
+        return remote(total_buf.at[here], total_buf.at[here], z_send.at[3, t], z_recv.at[3, at], target, x)
+
+    def back_y():
+        here = span(four_at, four)
+        return hand(3, total_buf.at[here], total_buf.at[here], across, x)
+
+    def back_core():
+        here = side_rows(c, both)
+        return hand(4, total_buf.at[here], total_buf.at[here], sibling, x)
+
+    def share_gram():
+        here = side_rows(c, part)
+        return hand(5, work.at[here], work.at[here], sibling, x)
 
     def block(side, core, h):
         at = pl.ds(pl.multiple_of((2 * side + core) * rows, rows), rows)
@@ -302,25 +295,68 @@
             own_copy(source).wait_recv()
 
     first(0)
+    trade_gram.wait()
+    here = side_rows(c, part)
+    work[here, :] = (gram_buf[0, here, :] + gram_buf[1, here, :]) / order
+    share_gram().start()
     first(1)
+    second(0)
+    ones = lax.broadcasted_iota(jnp.int32, (rank, rank), 0) == lax.broadcasted_iota(jnp.int32, (rank, rank), 1)
+    inverse[...] = ones.astype(jnp.float32)
+    share_gram().wait()
     eliminate(work, inverse, 0)
-    second(0)
     second(1)
+
+    old_high, old_low = split(new_ref_scaled(factor_ref))
+    meet_high, meet_low = split(range_buf[...])
+    applied_high, applied_low = split(nn(old_high, meet_high) + nn(old_low, meet_high) + nn(old_high, meet_low))
+
+    @pl.when(theirs)
+    def _():
+        give_range.wait_recv()
+
+    own_high, own_low = split(own_range[...])
+    term = tn(own_high, applied_high) + tn(own_low, applied_high) + tn(own_high, applied_low)
+    trade_thin.wait()
+    thin_high, thin_low = split(jnp.where(x == 0, thin_buf[2] + thin_buf[3], 0.0))
+    term_buf[...] = term + tn(thin_high, thin_high) + tn(thin_high, thin_low) + tn(thin_low, thin_high)
+    sum_core().start()
     eliminate(work, inverse, 1)
-    loop(lambda k: scatter(k, 0).wait_recv())
-    total_buf[rows_of(me), :] = jnp.sum(parts[...], axis=0)
-    loop(lambda k: spread(k, None).start())
-    for k in range(2, rank // NB):
+    sum_core().wait()
+    here = side_rows(c, both)
+    term_buf[here, :] += parts[0:both, :]
+    sum_y().start()
+    third(0)
+    sum_y().wait()
+    here = span(four_at, four)
+    term_buf[here, :] += parts[both:both + four, :]
+    sum_x().start()
+    eliminate(work, inverse, 2)
+    sum_x().wait()
+    total_buf[here, :] = term_buf[here, :] + parts[both + four:both + 2 * four, :]
+    term_buf[here, :] = total_buf[here, :]
+    for k in peers:
+        sum_z(k, True).start()
+    summed = term_buf[span(four_at + z * fine, fine), :]
+    for k in peers:
+        sum_z(k, False).wait_recv()
+        summed = summed + parts[span(both + 2 * four + line(k)[0] * fine, fine), :]
+    total_buf[span(four_at + z * fine, fine), :] = summed
+    for k in peers:
+        back_z(k, True).start()
+    for k in range(3, rank // NB):
         eliminate(work, inverse, k)
-    third(0)
-    third(1)
+    for k in peers:
+        back_z(k, False).wait_recv()
+    back_y().start()
     whole = inverse[...]
     basis_ref[...] = nt(own_range[...], whole, HIGHEST)
-    loop(lambda k: spread(k, 0).wait_recv())
+    back_y().wait()
+    back_core().start()
+    third(1)
+    back_core().wait()
     core_ref[...] = nt(nn(whole, total_buf[...], HIGHEST), whole, HIGHEST) / order
 
-    loop(lambda k: scatter(k, 0).wait_send())
-    loop(lambda k: spread(k, None).wait_send())
     for h in range(2):
         core_copy(h).wait_send()
         y_copy(h).wait_send()
@@ -329,6 +365,8 @@
     for k in peers:
         line_reduce(k, True).wait_send()
         line_gather(k, True).wait_send()
+        sum_z(k, True).wait_send()
+        back_z(k, True).wait_send()
 
     @pl.when(mine)
     def _():
@@ -347,11 +385,17 @@
     row_id = lax.broadcasted_iota(jnp.int32, (size, size), 0)
     eye = row_id == lax.broadcasted_iota(jnp.int32, (size, size), 1)
     both = jnp.concatenate([block, eye.astype(jnp.float32)], axis=1)
-    ids = lax.broadcasted_iota(jnp.int32, (size, 1), 0)
-    for j in range(size - 1):
-        row = both[j:j + 1, :] * (1.0 / both[j:j + 1, j:j + 1])
-        column = jnp.where(ids > j, both[:, j:j + 1], 0.0)
-        both = both - column * row
+    ids = lax.broadcasted_iota(jnp.int32, both.shape, 0)
+    width = 8
+    for p in range(0, size, width):
+        columns = [jnp.broadcast_to(both[:, p + i:p + i + 1], both.shape) for i in range(width)]
+        for i in range(width):
+            j = p + i
+            scale = 1.0 / columns[i][j:j + 1, :]
+            below = jnp.where(ids > j, columns[i], 0.0)
+            for k in range(i + 1, width):
+                columns[k] = columns[k] - below * (columns[i][p + k:p + k + 1, :] * scale)
+            both = both - below * (both[j:j + 1, :] * scale)
     pivot = jnp.sum(jnp.where(eye, both[:, :size], 0.0), axis=1, keepdims=True)
     return both[:, size:] / jnp.sqrt(pivot)
 
@@ -376,7 +420,7 @@
     vmem = pl.BlockSpec(memory_space=pltpu.VMEM)
     shape = jax.ShapeDtypeStruct
     dma = pltpu.SemaphoreType.DMA
-    everyone, nz, half = 2 * n, n // 4, cols // 2
+    nz, half = n // 4, cols // 2
     return pl.pallas_call(
         functools.partial(main_kernel, n),
         out_shape=(shape((rows, cols), f32), shape((rows, rank), f32), shape((rank, rank), f32)),
@@ -394,7 +438,7 @@
             pltpu.VMEM((rows, rank), f32),
             pltpu.VMEM((2, rank, rank), f32),
             pltpu.VMEM((rank, rank), f32),
-            pltpu.VMEM((everyone, rank // everyone, rank), f32),
+            pltpu.VMEM((2 * rank, rank), f32),
             pltpu.VMEM((rank, rank), f32),
             pltpu.VMEM((rank, rank), f32),
             pltpu.VMEM((rank, rank), f32),
@@ -403,8 +447,8 @@
             pltpu.VMEM((2, rows, half), f32),
             pltpu.VMEM((2, rows, half), f32),
             dma((2, 2 * nz)), dma((2 * nz,)), dma((nz,)), dma((nz,)), dma((5,)), dma((5,)), dma((4,)), dma((4,)),
-            dma((2, nz)), dma((2, nz)), dma((2,)), dma((2,)), dma((2,)), dma((2,)),
-            dma((everyone,)), dma((everyone,)), dma((everyone,)), dma((everyone,)), dma((2,)),
+            dma((4, nz)), dma((4, nz)), dma((2,)), dma((2,)), dma((2,)), dma((2,)),
+            dma((6,)), dma((6,)), dma((2,)),
         ],
         compiler_params=pltpu.CompilerParams(collective_id=0, has_side_effects=True, vmem_limit_bytes=VMEM_BYTES),
     )(factor, gradient, sketch_ids)
@@ -444,7 +488,7 @@
         rows, cols = factor.shape
         rank = sketch_ids.shape[1]
         fits = (halves == 2 and n == 16 and rows % 64 == 0 and cols == 8 * rows
-                and rank % (16 * n) == 0 and rank % NB == 0)
+                and rank % (8 * n) == 0 and rank % NB == 0 and gradient.shape[1] % 16 == 0)
         return (fast if fits else plain)(n, factor, gradient, sketch_ids)
 
     return jax.shard_map(

time: 149 us -> 152 us (1.020)
  the two profiles are of different devices: /device:TPU:24 before, /device:TPU:0 now
where the time goes in v4:
time: 152 us
  Pallas kernels  146 us (96%)
  local copies, waits for them, and re-layouts  5.12 us (3%)
    pallas_call x1, Pallas kernels, fast(): pl.pallas_call(functools.partial(main_kernel, n), out_shape=(shape((rows,...  146 us
    unnamed x4, local copies, waits for them, and re-layouts  5.12 us

profile of v4, /device:TPU:0, one launch (start us, length us, event | category | flops | bytes accessed | tf_op | source)
XLA Modules:
  0.0 151.9 jit_solution(15835909825467311950)
XLA Ops:
  0.6 1.4 copy.6.grad_ref
  2.0 146.1 %shard_map.58 = (f32[192,1536]{1,0:T(8,128)}, f32[192,256]{1,0:T(8,128)S(1)}, f32[256,256]{1,0:T(8,128)S(1)}) custom-call(f32[192,1536]{1,0:T(8,128)} %factor_ref.1, bf16[1536,240]{1,0:T(8,128)(2,1)S(1)} %copy.6.grad_ref, s32[1536,256]{1,0:T(8,128)} %sketch_ref.1), custom_call_target="tpu_custom_call" | custom-call | tf_op jit(solution)/shard_map/pallas_call | solution.py:424
  148.1 2.4 %copy.10 = f32[192,1536]{1,0:T(8,128)} copy(f32[192,1536]{1,0:T(8,128)} %get-tuple-element.6) | data formatting | bytes 2359296
  150.5 0.7 copy.11
  151.2 0.7 copy.12

commit v5 on v4

--- a/solution.py
+++ b/solution.py
@@ -385,17 +385,11 @@
     row_id = lax.broadcasted_iota(jnp.int32, (size, size), 0)
     eye = row_id == lax.broadcasted_iota(jnp.int32, (size, size), 1)
     both = jnp.concatenate([block, eye.astype(jnp.float32)], axis=1)
-    ids = lax.broadcasted_iota(jnp.int32, both.shape, 0)
-    width = 8
-    for p in range(0, size, width):
-        columns = [jnp.broadcast_to(both[:, p + i:p + i + 1], both.shape) for i in range(width)]
-        for i in range(width):
-            j = p + i
-            scale = 1.0 / columns[i][j:j + 1, :]
-            below = jnp.where(ids > j, columns[i], 0.0)
-            for k in range(i + 1, width):
-                columns[k] = columns[k] - below * (columns[i][p + k:p + k + 1, :] * scale)
-            both = both - below * (both[j:j + 1, :] * scale)
+    ids = lax.broadcasted_iota(jnp.int32, (size, 1), 0)
+    for j in range(size - 1):
+        row = both[j:j + 1, :] * (1.0 / both[j:j + 1, j:j + 1])
+        column = jnp.where(ids > j, both[:, j:j + 1], 0.0)
+        both = both - column * row
     pivot = jnp.sum(jnp.where(eye, both[:, :size], 0.0), axis=1, keepdims=True)
     return both[:, size:] / jnp.sqrt(pivot)
 

time: 152 us -> 159 us (1.046)
  Pallas kernels: 146 us -> 153 us
    pallas_call x1, Pallas kernels: 146 us -> 153 us  [fast(): pl.pallas_call(functools.partial(main_kernel, n), out_shape=(shape((rows,...]
where the time goes in v5:
time: 159 us
  Pallas kernels  153 us (96%)
  local copies, waits for them, and re-layouts  5.12 us (3%)
    pallas_call x1, Pallas kernels, fast(): pl.pallas_call(functools.partial(main_kernel, n), out_shape=(shape((rows,...  153 us
    unnamed x4, local copies, waits for them, and re-layouts  5.12 us

profile of v5, /device:TPU:0, one launch (start us, length us, event | category | flops | bytes accessed | tf_op | source)
XLA Modules:
  0.0 158.7 jit_solution(3021851992980129935)
XLA Ops:
  0.6 1.4 copy.6.grad_ref
  2.0 152.9 %shard_map.58 = (f32[192,1536]{1,0:T(8,128)}, f32[192,256]{1,0:T(8,128)S(1)}, f32[256,256]{1,0:T(8,128)S(1)}) custom-call(f32[192,1536]{1,0:T(8,128)} %factor_ref.1, bf16[1536,240]{1,0:T(8,128)(2,1)S(1)} %copy.6.grad_ref, s32[1536,256]{1,0:T(8,128)} %sketch_ref.1), custom_call_target="tpu_custom_call" | custom-call | tf_op jit(solution)/shard_map/pallas_call | solution.py:418
  154.9 2.4 %copy.10 = f32[192,1536]{1,0:T(8,128)} copy(f32[192,1536]{1,0:T(8,128)} %get-tuple-element.6) | data formatting | bytes 2359296
  157.3 0.7 copy.11
  158.0 0.7 copy.12
